TPU v7x, 32 devices: a whole 2x2x4 slice. The times are simulated.
32 devices in a mesh: grp: 2 (over x), gz: 8 (over z, y), gy: 2 (over core).
Axes of the slice: x: 2, y: 2, z: 4, core: 2. Of those that a mesh axis runs over, the one named last changes fastest.
Arguments:
- density: float32 [256, 64, 1024], P(('grp', 'gz'), 'gy'), parts along dimension 0, may hold values from 0.05 to 17
- bin_exponents: int32 [3], replicated, may hold values from -2 to 2
- writer_table: int32 [3, 8], replicated, may hold values from 0 to 7, each once within a row
Outputs:
- coarse_grid: float32 [32, 8, 128], P(('grp', 'gz'), 'gy'), parts along dimension 0
- finest_coefficients: bfloat16 [16, 2, 8, 65536], P(('grp', 'gz'), 'gy'), parts along dimension 0
- middle_coefficients: bfloat16 [16, 2, 8, 8192], P(('grp', 'gz'), 'gy'), parts along dimension 0
- coarser_coefficients: bfloat16 [16, 2, 8, 1024], P(('grp', 'gz'), 'gy'), parts along dimension 0
There are 2 independent parts, one for each index of `grp`. A program takes and returns all parts, laid end to end along the dimension named above; an argument that names none is the same for every part. Nothing has to cross between parts.
Inputs may be any that keep to these rules, and one draw needn't show every extreme that they name: Each row of writer_table names every writer 0 to 7 once.
All inputs are finite; a program needn't handle non-finite values.
Results may differ from a plain program's by a relative error of at most 0.00115.
Values may be sent and summed in bfloat16 or wider, within the bound.
A program may use at most 128 MiB of HBM per device.

v0:
```python
import jax
import jax.numpy as jnp
from jax import lax
from jax.sharding import PartitionSpec as P

LEVELS = 3
SWEEPS = 2


def extended_2(value, sides, width):
    for axis, dim in sides:
        peers, length = (lax.axis_size(axis), value.shape[dim])
        up = [(i, (i + 1) % peers) for i in range(peers - 1)]
        down = [(j, i) for i, j in up]
        last = lax.slice_in_dim(value, length - width, length, axis=dim)
        initial = lax.slice_in_dim(value, 0, width, axis=dim)
        before = lax.ppermute(last, axis, up)
        after = lax.ppermute(initial, axis, down)
        value = jnp.concatenate([before, value, after], axis=dim)
    return value


def passed_along(value, axis, steps):
    count = lax.axis_size(axis)
    initial, last = (max(0, -steps), min(count, count - steps))
    return lax.ppermute(value, axis, [(source, source + steps) for source in range(initial, last)])


def upsample(values, dim_index):
    length = values.shape[dim_index] - 1
    lower_part = lax.slice_in_dim(values, 0, length, axis=dim_index)
    upper_part = lax.slice_in_dim(values, 1, length + 1, axis=dim_index)
    middle = (lower_part + upper_part) * 0.5
    stacked = jnp.stack((lower_part, middle), axis=dim_index + 1)
    new_shape = values.shape[:dim_index] + (2 * length,) + values.shape[dim_index + 1 :]
    return stacked.reshape(new_shape)


def interpolate(extended):
    widened = jnp.pad(extended, ((0, 0), (0, 0), (0, 1)))
    widened = upsample(widened, 2)
    widened = upsample(widened, 1)
    return upsample(widened, 0)


def restrict(padded, dim_index):
    length = (padded.shape[dim_index] - 4) // 2
    weights = (1.0 / 12.0, 0.5, 5.0 / 6.0, 0.5, 1.0 / 12.0)
    running = lax.slice_in_dim(padded, 0, 2 * length - 1, stride=2, axis=dim_index) * weights[0]
    for offset in range(1, 5):
        shifted = lax.slice_in_dim(
            padded, offset, offset + 2 * length - 1, stride=2, axis=dim_index
        )
        running = running + shifted * weights[offset]
    return running


def project_load(padded):
    running = restrict(padded, 2)
    running = restrict(running, 1)
    return restrict(running, 0)


def solve_line(target, dim_index, padder):
    length = target.shape[dim_index]
    iterate = target * 0.75
    for sweep_index in range(SWEEPS):
        padded = padder(iterate)
        lower_part = lax.slice_in_dim(padded, 0, length, axis=dim_index)
        upper_part = lax.slice_in_dim(padded, 2, length + 2, axis=dim_index)
        iterate = (target - (lower_part + upper_part) * (1.0 / 3.0)) * 0.75
    return iterate


def pad_lines(values):
    return jnp.pad(values, ((0, 0), (0, 0), (1, 1)))


def across_rows(values):
    return extended_2(values, (("gy", 1),), 1)


def across_planes(values):
    return extended_2(values, (("gz", 0),), 1)


def inverse_of(row):
    writer_ids = jnp.arange(row.shape[0], dtype=jnp.int32)
    matches = (row[None, :] == writer_ids[:, None]).astype(jnp.int32)
    return jnp.sum(matches * writer_ids[None, :], axis=1)


def reorder(quantized, row):
    pieces = quantized.reshape(row.shape[0], -1)
    return jnp.take(pieces, inverse_of(row), axis=0)[None, None]


def shards(density, bin_exponents, writer_table):
    current = density
    received = []
    for depth_index in range(LEVELS):
        coarse_nodes = current[::2, ::2, ::2]
        rim_row = passed_along(coarse_nodes[:, 0:1, :], "gy", -1)
        extended = jnp.concatenate((coarse_nodes, rim_row), axis=1)
        rim_plane = passed_along(extended[0:1], "gz", -1)
        extended = jnp.concatenate((extended, rim_plane), axis=0)
        details = current - interpolate(extended)
        padded = extended_2(details, (("gz", 0), ("gy", 1)), 2)
        load_term = project_load(jnp.pad(padded, ((0, 0), (0, 0), (2, 2))))
        correction = solve_line(load_term, 2, pad_lines)
        correction = solve_line(correction, 1, across_rows)
        correction = solve_line(correction, 0, across_planes)
        current = coarse_nodes + correction
        bin_scale = jnp.exp2(-bin_exponents[depth_index].astype(jnp.float32))
        quantized = (details * bin_scale).astype(jnp.bfloat16)
        message = reorder(quantized, writer_table[depth_index])
        received.append(lax.all_to_all(message, "gz", split_axis=2, concat_axis=2, tiled=True))
    return (current, received[0], received[1], received[2])


def solution(mesh):
    in_specs = (P(("grp", "gz"), "gy", None), P(), P())
    out_specs = (
        P(("grp", "gz"), "gy", None),
        P(("grp", "gz"), "gy", None, None),
        P(("grp", "gz"), "gy", None, None),
        P(("grp", "gz"), "gy", None, None),
    )
    return jax.shard_map(shards, mesh=mesh, in_specs=in_specs, out_specs=out_specs, check_vma=False)
```

profile of v0, /device:TPU:0, one launch (start us, length us, event | category | flops | bytes accessed | tf_op | source)
XLA Modules:
  0.0 586.9 jit_solution(3275088633194609802)
XLA Ops:
  0.6 10.1 %slice.480 = f32[8,16,512]{2,1,0:T(8,128)S(1)} slice(f32[16,32,1024]{2,1,0:T(8,128)} %param.3), slice={[0:16:2], [0:32:2], [0:1024:2]} | slice | bytes 524288 | tf_op jit(solution)/shard_map/slice | solution.py:102
  21.2 4.8 copy.58
  26.0 5.2 slice_bitcast_fusion
  31.3 6.4 %fusion = (f32[8,16,2,1024]{1,3,0,2:T(8,128)}, f32[8,16,2,1024]{1,3,0,2:T(8,128)}) fusion(f32[9,16,1,1024]{1,3,0,2:T(8,128)S(1)} %get-tuple-element.38, f32[9,16,1,1024]{1,3,0,2:T(8,128)S(1)} %get-tuple-element.39), kind=kLoop, calls=%fused_computation.5 | loop fusion | flops 524288 | bytes 3276800 | tf_op jit(solution)/shard_map/stack | solution.py:34
  37.7 5.3 copy.59
  43.0 5.3 copy.60
  52.1 4.8 collective-permute-start.2
  58.2 9.0 %collective-permute-done.2 = f32[2,32,1024]{2,1,0:T(8,128)S(1)} collective-permute-done((f32[2,32,1024]{2,1,0:T(8,128)S(1)}, f32[2,32,1024]{2,1,0:T(8,128)S(1)}, u32[]{:S(2)}, u32[]{:S(2)}) %collective-permute-start.2) | collective-permute-done | bytes 262176 | tf_op jit(solution)/shard_map/ppermute | solution.py:17
  72.0 5.1 select_maximum_fusion
  77.1 50.1 %slice.493 = f32[20,36,512]{2,1,0:T(8,128)S(1)} slice(f32[20,36,1028]{2,1,0:T(8,128)} %select_maximum_fusion), slice={[0:20:1], [0:36:1], [0:1023:2]} | slice | bytes 2949120 | tf_op jit(solution)/shard_map/slice | solution.py:49
  127.1 50.5 %slice.494 = f32[20,36,512]{2,1,0:T(8,128)} slice(f32[20,36,1028]{2,1,0:T(8,128)} %select_maximum_fusion), slice={[0:20:1], [0:36:1], [1:1024:2]} | slice | bytes 2949120 | tf_op jit(solution)/shard_map/slice | solution.py:51
  177.7 50.8 %slice.495 = f32[20,36,512]{2,1,0:T(8,128)} slice(f32[20,36,1028]{2,1,0:T(8,128)} %select_maximum_fusion), slice={[0:20:1], [0:36:1], [2:1025:2]} | slice | bytes 2949120 | tf_op jit(solution)/shard_map/slice | solution.py:51
  228.5 50.5 %slice.496 = f32[20,36,512]{2,1,0:T(8,128)} slice(f32[20,36,1028]{2,1,0:T(8,128)} %select_maximum_fusion), slice={[0:20:1], [0:36:1], [3:1026:2]} | slice | bytes 2949120 | tf_op jit(solution)/shard_map/slice | solution.py:51
  279.0 50.9 %slice.497 = f32[20,36,512]{2,1,0:T(8,128)} slice(f32[20,36,1028]{2,1,0:T(8,128)} %select_maximum_fusion), slice={[0:20:1], [0:36:1], [4:1027:2]} | slice | bytes 2949120 | tf_op jit(solution)/shard_map/slice | solution.py:51
  359.9 4.6 collective-permute-done.11
  364.6 4.8 collective-permute-start.12
  405.1 10.7 %slice.541 = f32[12,20,256]{2,1,0:T(8,128)S(1)} slice(f32[12,20,516]{2,1,0:T(8,128)S(1)} %select_maximum_fusion.4), slice={[0:12:1], [0:20:1], [0:511:2]} | slice | bytes 491520 | tf_op jit(solution)/shard_map/slice | solution.py:49
  415.8 10.5 %slice.542 = f32[12,20,256]{2,1,0:T(8,128)S(1)} slice(f32[12,20,516]{2,1,0:T(8,128)S(1)} %select_maximum_fusion.4), slice={[0:12:1], [0:20:1], [1:512:2]} | slice | bytes 491520 | tf_op jit(solution)/shard_map/slice | solution.py:51
  426.3 10.5 %slice.543 = f32[12,20,256]{2,1,0:T(8,128)S(1)} slice(f32[12,20,516]{2,1,0:T(8,128)S(1)} %select_maximum_fusion.4), slice={[0:12:1], [0:20:1], [2:513:2]} | slice | bytes 491520 | tf_op jit(solution)/shard_map/slice | solution.py:51
  436.8 10.7 %slice.544 = f32[12,20,256]{2,1,0:T(8,128)S(1)} slice(f32[12,20,516]{2,1,0:T(8,128)S(1)} %select_maximum_fusion.4), slice={[0:12:1], [0:20:1], [3:514:2]} | slice | bytes 491520 | tf_op jit(solution)/shard_map/slice | solution.py:51
  447.5 10.5 %slice.545 = f32[12,20,256]{2,1,0:T(8,128)S(1)} slice(f32[12,20,516]{2,1,0:T(8,128)S(1)} %select_maximum_fusion.4), slice={[0:12:1], [0:20:1], [4:515:2]} | slice | bytes 491520 | tf_op jit(solution)/shard_map/slice | solution.py:51
  496.2 7.0 %reduce = bf16[8,65536]{1,0:T(8,128)(2,1)S(1)} reduce(bf16[8,1,1,65536]{3,2,1,0:T(2,128)(2,1)S(1)} %bitcast.108, bf16[]{:T(256)} %broadcast.453), dimensions={1,2}, to_apply=%bitcast.93.reduce_sub_computation | reduce | bytes 2097154
  536.1 6.0 %all-to-all-start.1 = ((bf16[8,2,4096]{2,1,0:T(2,128)(2,1)}), bf16[8,2,4096]{2,1,0:T(2,128)(2,1)S(1)}, u32[]{:S(2)}, u32[]{:S(2)}) async-start(bf16[8,2,4096]{2,1,0:T(2,128)(2,1)} %reshape.280), calls=%async_computation.1 | async-start | bytes 262144 | tf_op jit(solution)/shard_map/all_to_all | solution.py:117
  542.2 7.6 %all-to-all-done.1 = bf16[8,2,4096]{2,1,0:T(2,128)(2,1)S(1)} async-done(((bf16[8,2,4096]{2,1,0:T(2,128)(2,1)}), bf16[8,2,4096]{2,1,0:T(2,128)(2,1)S(1)}, u32[]{:S(2)}, u32[]{:S(2)}) %all-to-all-start.1) | async-done | bytes 131104 | tf_op jit(solution)/shard_map/all_to_all | solution.py:117
  (237 shorter events, 190.6 us)
Async XLA Ops:
  13.9 6.9 %collective-permute-start.1 = (f32[1,17,512]{2,1,0:T(8,128)S(1)}, f32[1,17,512]{2,1,0:T(8,128)S(1)}, u32[]{:S(2)}, u32[]{:S(2)}) collective-permute-start(f32[1,17,512]{2,1,0:T(8,128)S(1)} %pad_maximum_fusion.22), channel_id=1, source_target_pairs={{2,0},{4,2},{6,4},{8,6},{10,8},{12,10},{14,12},{3,1},{5,3},{7,5},{... | collective-permute-start | bytes 104456 | tf_op jit(solution)/shard_map/ppermute | solution.py:26
  52.1 15.2 %collective-permute-start.2 = (f32[2,32,1024]{2,1,0:T(8,128)S(1)}, f32[2,32,1024]{2,1,0:T(8,128)S(1)}, u32[]{:S(2)}, u32[]{:S(2)}) collective-permute-start(f32[2,32,1024]{2,1,0:T(8,128)S(1)} %get-tuple-element.42), channel_id=1, source_target_pairs={{0,2},{2,4},{4,6},{6,8},{8,10},{10,12},{12,14},{1,3},{3,5},{5,7},{... | collective-permute-start | bytes 786440 | tf_op jit(solution)/shard_map/ppermute | solution.py:17
  56.9 10.3 %collective-permute-start.3 = (f32[2,32,1024]{2,1,0:T(8,128)S(1)}, f32[2,32,1024]{2,1,0:T(8,128)S(1)}, u32[]{:S(2)}, u32[]{:S(2)}) collective-permute-start(f32[2,32,1024]{2,1,0:T(8,128)S(1)} %get-tuple-element.43), channel_id=1, source_target_pairs={{2,0},{4,2},{6,4},{8,6},{10,8},{12,10},{14,12},{3,1},{5,3},{7,5},{... | collective-permute-start | bytes 786440 | tf_op jit(solution)/shard_map/ppermute | solution.py:18
  353.9 6.0 %collective-permute-start.10 = (f32[1,16,512]{2,1,0:T(8,128)S(1)}, f32[1,16,512]{2,1,0:T(8,128)S(1)}, u32[]{:S(2)}, u32[]{:S(2)}) collective-permute-start(f32[1,16,512]{2,1,0:T(8,128)S(1)} %get-tuple-element.56), channel_id=1, source_target_pairs={{0,2},{2,4},{4,6},{6,8},{8,10},{10,12},{12,14},{1,3},{3,5},{5,7},{... | collective-permute-start | bytes 98312 | tf_op jit(solution)/shard_map/ppermute | solution.py:17
  358.3 6.2 %collective-permute-start.11 = (f32[1,16,512]{2,1,0:T(8,128)S(1)}, f32[1,16,512]{2,1,0:T(8,128)S(1)}, u32[]{:S(2)}, u32[]{:S(2)}) collective-permute-start(f32[1,16,512]{2,1,0:T(8,128)S(1)} %get-tuple-element.57), channel_id=1, source_target_pairs={{2,0},{4,2},{6,4},{8,6},{10,8},{12,10},{14,12},{3,1},{5,3},{7,5},{... | collective-permute-start | bytes 98312 | tf_op jit(solution)/shard_map/ppermute | solution.py:18
  364.6 6.4 %collective-permute-start.12 = (f32[1,16,512]{2,1,0:T(8,128)S(1)}, f32[1,16,512]{2,1,0:T(8,128)S(1)}, u32[]{:S(2)}, u32[]{:S(2)}) collective-permute-start(f32[1,16,512]{2,1,0:T(8,128)S(1)} %get-tuple-element.54), channel_id=1, source_target_pairs={{0,2},{2,4},{4,6},{6,8},{8,10},{10,12},{12,14},{1,3},{3,5},{5,7},{... | collective-permute-start | bytes 98312 | tf_op jit(solution)/shard_map/ppermute | solution.py:17
  369.4 5.8 collective-permute-start.13
  379.8 5.6 collective-permute-start.15
  390.2 5.7 collective-permute-start.16
  394.1 6.2 %collective-permute-start.17 = (f32[2,16,512]{2,1,0:T(8,128)S(1)}, f32[2,16,512]{2,1,0:T(8,128)S(1)}, u32[]{:S(2)}, u32[]{:S(2)}) collective-permute-start(f32[2,16,512]{2,1,0:T(8,128)S(1)} %get-tuple-element.53), channel_id=1, source_target_pairs={{2,0},{4,2},{6,4},{8,6},{10,8},{12,10},{14,12},{3,1},{5,3},{7,5},{... | collective-permute-start | bytes 196616 | tf_op jit(solution)/shard_map/ppermute | solution.py:18
  469.1 5.3 collective-permute-start.24
  473.0 5.5 collective-permute-start.25
  482.4 5.5 collective-permute-start.27
  492.2 13.6 %collective-permute-start.29 = (f32[1,5,128]{2,1,0:T(8,128)S(1)}, f32[1,5,128]{2,1,0:T(8,128)S(1)}, u32[]{:S(2)}, u32[]{:S(2)}) collective-permute-start(f32[1,5,128]{2,1,0:T(8,128)S(1)} %pad_maximum_fusion.47), channel_id=1, source_target_pairs={{2,0},{4,2},{6,4},{8,6},{10,8},{12,10},{14,12},{3,1},{5,3},{7,5},{... | collective-permute-start | bytes 7688 | tf_op jit(solution)/shard_map/ppermute | solution.py:26
  506.8 8.9 %collective-permute-start.30 = (f32[2,8,256]{2,1,0:T(8,128)S(1)}, f32[2,8,256]{2,1,0:T(8,128)S(1)}, u32[]{:S(2)}, u32[]{:S(2)}) collective-permute-start(f32[2,8,256]{2,1,0:T(8,128)S(1)} %get-tuple-element.68), channel_id=1, source_target_pairs={{0,2},{2,4},{4,6},{6,8},{8,10},{10,12},{12,14},{1,3},{3,5},{5,7},{... | collective-permute-start | bytes 49160 | tf_op jit(solution)/shard_map/ppermute | solution.py:17
  511.4 6.6 %collective-permute-start.31 = (f32[2,8,256]{2,1,0:T(8,128)S(1)}, f32[2,8,256]{2,1,0:T(8,128)S(1)}, u32[]{:S(2)}, u32[]{:S(2)}) collective-permute-start(f32[2,8,256]{2,1,0:T(8,128)S(1)} %get-tuple-element.69), channel_id=1, source_target_pairs={{2,0},{4,2},{6,4},{8,6},{10,8},{12,10},{14,12},{3,1},{5,3},{7,5},{... | collective-permute-start | bytes 49160 | tf_op jit(solution)/shard_map/ppermute | solution.py:18
  518.0 9.2 %collective-permute-start.32 = (f32[8,2,256]{2,1,0:T(2,128)S(1)}, f32[8,2,256]{2,1,0:T(2,128)S(1)}, u32[]{:S(2)}, u32[]{:S(2)}) collective-permute-start(f32[8,2,256]{2,1,0:T(2,128)S(1)} %get-tuple-element.64), channel_id=1, source_target_pairs={{0,1},{2,3},{4,5},{6,7},{8,9},{10,11},{12,13},{14,15},{16,17},{18,... | collective-permute-start | bytes 49160 | tf_op jit(solution)/shard_map/ppermute | solution.py:17
  519.9 7.3 %collective-permute-start.33 = (f32[8,2,256]{2,1,0:T(2,128)S(1)}, f32[8,2,256]{2,1,0:T(2,128)S(1)}, u32[]{:S(2)}, u32[]{:S(2)}) collective-permute-start(f32[8,2,256]{2,1,0:T(2,128)S(1)} %get-tuple-element.65), channel_id=1, source_target_pairs={{1,0},{3,2},{5,4},{7,6},{9,8},{11,10},{13,12},{15,14},{17,16},{19,... | collective-permute-start | bytes 49160 | tf_op jit(solution)/shard_map/ppermute | solution.py:18
  522.7 13.4 %all-to-all-start.2 = ((bf16[8,2,512]{2,1,0:T(2,128)(2,1)}), bf16[8,2,512]{2,1,0:T(2,128)(2,1)S(1)}, u32[]{:S(2)}, u32[]{:S(2)}) async-start(bf16[8,2,512]{2,1,0:T(2,128)(2,1)} %reshape.282), calls=%async_computation.2 | async-start | bytes 32768 | tf_op jit(solution)/shard_map/all_to_all | solution.py:117
  536.1 13.7 %all-to-all-start.1 = ((bf16[8,2,4096]{2,1,0:T(2,128)(2,1)}), bf16[8,2,4096]{2,1,0:T(2,128)(2,1)S(1)}, u32[]{:S(2)}, u32[]{:S(2)}) async-start(bf16[8,2,4096]{2,1,0:T(2,128)(2,1)} %reshape.280), calls=%async_computation.1 | async-start | bytes 262144 | tf_op jit(solution)/shard_map/all_to_all | solution.py:117
  549.8 33.8 %all-to-all-start = ((bf16[8,2,32768]{2,1,0:T(2,128)(2,1)}), bf16[8,2,32768]{2,1,0:T(2,128)(2,1)S(1)}, u32[]{:S(2)}, u32[]{:S(2)}) async-start(bf16[8,2,32768]{2,1,0:T(2,128)(2,1)} %reshape.278), calls=%async_computation | async-start | bytes 2097152 | tf_op jit(solution)/shard_map/all_to_all | solution.py:117
  566.8 5.5 collective-permute-start.39
  572.3 6.2 %collective-permute-start.40 = (f32[1,4,128]{2,1,0:T(4,128)S(1)}, f32[1,4,128]{2,1,0:T(4,128)S(1)}, u32[]{:S(2)}, u32[]{:S(2)}) collective-permute-start(f32[1,4,128]{2,1,0:T(4,128)S(1)} %get-tuple-element.82), channel_id=1, source_target_pairs={{0,2},{2,4},{4,6},{6,8},{8,10},{10,12},{12,14},{1,3},{3,5},{5,7},{... | collective-permute-start | bytes 6152 | tf_op jit(solution)/shard_map/ppermute | solution.py:17
  576.6 5.5 collective-permute-start.41
  (24 other events, 113.2 us)
where the time goes:
time: 597 us; the launch traced here: 587 us
  local copies, waits for them, and re-layouts  369 us (62%)
  starting transfers between devices  100 us (17%)
  waiting for transfers between devices  73.9 us (12%)
  other arithmetic  39.8 us (7%)
    slice x24, local copies, waits for them, and re-layouts, restrict(): lax.slice_in_dim(padded, offset, offset + 2 * length - 1, stride=2, axis=...  259 us
    slice x6, local copies, waits for them, and re-layouts, restrict(): lax.slice_in_dim(padded, 0, 2 * length - 1, stride=2, axis=dim_index)  62.8 us
    ppermute x18, starting transfers between devices, extended_2(): before = lax.ppermute(last, axis, up)  54.4 us
    ppermute x18, waiting for transfers between devices, extended_2(): after = lax.ppermute(initial, axis, down)  45.4 us
    ppermute x18, starting transfers between devices, extended_2(): after = lax.ppermute(initial, axis, down)  23.4 us
    another operation x18, other arithmetic, upsample(): stacked = jnp.stack((lower_part, middle), axis=dim_index + 1)  14.2 us
    all_to_all x3, starting transfers between devices, shards(): lax.all_to_all(message, 'gz', split_axis=2, concat_axis=2, tiled=True)  14.1 us
    slice x3, local copies, waits for them, and re-layouts, shards(): coarse_nodes = current[::2, ::2, ::2]  12 us
  transfers between devices with their start and end apart: 45, of which 25 were waited for; matrix products, arithmetic and copies ran while one was open for 5% of the time, Pallas kernels for 0%

commit v1 on v0

v1 whole, which is shorter than its diff:
```python
import functools

import jax
import jax.numpy as jnp
import numpy as np
from jax import lax
from jax.experimental import pallas as pl
from jax.experimental.pallas import tpu as pltpu
from jax.sharding import PartitionSpec as P

LEVELS = 3
SWEEPS = 2
BF16 = jnp.bfloat16
F32 = jnp.float32


def line_operator(count):
    half = count // 2
    restrict = np.zeros((half, count))
    for k in range(half):
        for off, weight in zip(range(-2, 3), (1 / 12, 0.5, 5 / 6, 0.5, 1 / 12)):
            if 0 <= 2 * k + off < count:
                restrict[k, 2 * k + off] = weight
    near = np.eye(half, k=1) + np.eye(half, k=-1)
    iterate = 0.75 * restrict
    for _ in range(SWEEPS):
        iterate = 0.75 * (restrict - near @ iterate / 3)
    return iterate


def split_np(value):
    high = value.astype(np.float32).astype(BF16)
    low = (value - high.astype(np.float64)).astype(np.float32).astype(BF16)
    return np.stack([high, low])


def split(value):
    high = value.astype(BF16)
    return high, (value - high.astype(F32)).astype(BF16)


def dot3(left, right):
    (lh, ll), (rh, rl) = left, right
    dot = functools.partial(jnp.dot, preferred_element_type=F32)
    return dot(lh, rh) + dot(ll, rh) + dot(lh, rl)


class Plan:
    def __init__(self, depth, planes, rows, cols, peers):
        self.z, self.y, self.x = planes, rows, cols
        self.zc, self.yc, self.xc = planes // 2, rows // 2, cols // 2
        self.last = depth == LEVELS - 1
        self.kz = self.zc if self.last else self.zc + 1
        self.jy = self.yc if self.last else self.yc + 1
        self.br = 8 if self.last else self.yc + 8
        self.piece = planes * rows // peers
        self.packed = self.piece % 16 == 0
        self.blocks = {}
        total = 0
        for dz in (0, -1, 1, -2, 2):
            ks = [k for k in range(self.kz) if -3 <= k + dz * self.zc <= self.zc + 2]
            if not ks:
                continue
            for dy in (0, 1):
                height = self.br if dy == 0 else 8
                self.blocks[dz, dy] = (total, ks[0], len(ks), height)
                total += len(ks) * height
        self.m = total

    def messages(self):
        return [key for key in self.blocks if key != (0, 0)]

    def rows_matrix(self, peers, side):
        za, ya = line_operator(self.z * peers), line_operator(self.y * side)
        out = []
        for d in (0, peers // 2, peers - 1):
            for e in range(side):
                full = np.zeros((self.m, self.z * self.y))
                for (dz, dy), (start, first, count, height) in self.blocks.items():
                    dest = e if dy == 0 else 1 - e
                    base = 0 if dy == 0 or dest == 1 else self.yc - 3
                    span = self.jy if dy == 0 else (3 if dest == 1 else self.jy - base)
                    for i in range(count):
                        gk = (d + dz) * self.zc + first + i
                        if not 0 <= gk < self.zc * peers:
                            continue
                        zrow = za[gk, d * self.z:(d + 1) * self.z]
                        for j in range(span):
                            gj = dest * self.yc + base + j
                            if gj >= self.yc * side:
                                continue
                            yrow = ya[gj, e * self.y:(e + 1) * self.y]
                            full[start + i * height + j] = np.kron(zrow, yrow)
                out.append(split_np(full))
        return np.stack(out)


def kernel(plans, peers, density, scale, inverse, *refs):
    refs = list(refs)
    take = lambda count: [refs.pop(0) for _ in range(count)]
    row_hbm, col_w, sel_w = take(LEVELS), take(LEVELS), take(LEVELS)
    coarse_out = refs.pop(0)
    outs = take(LEVELS)
    curs, row_w, mids, flats, sends, prods, strips = (take(LEVELS) for _ in range(7))
    slots = [{key: refs.pop(0) for key in plan.messages()} for plan in plans]
    local_sem, rim_send, rim_recv, msg_send, msg_recv, a2a_send, a2a_recv = refs

    g, d, e = lax.axis_index("grp"), lax.axis_index("gz"), lax.axis_index("gy")
    variant = ((d + peers - 1) // peers + d // (peers - 1)) * 2 + e
    plan0 = plans[0]
    nz, ny = plan0.z, plan0.y

    loads = [pltpu.make_async_copy(density, curs[0].at[0:nz, 0:ny], local_sem.at[0])]
    for l in range(LEVELS):
        loads.append(pltpu.make_async_copy(row_hbm[l].at[variant], row_w[l], local_sem.at[1 + l]))
    for load in loads:
        load.start()

    barrier = pltpu.get_barrier_semaphore()
    for s in range(peers):
        for f in range(2):
            if (s, f) != (0, 0):
                pl.semaphore_signal(
                    barrier, inc=1, device_id=(g, lax.rem(d + s, peers), lax.rem(e + f, 2)),
                    device_id_type=pl.DeviceIdType.MESH)
    pl.semaphore_wait(barrier, 2 * peers - 1)

    def remote(src, dst, ssem, rsem, dz, de):
        return pltpu.make_async_remote_copy(
            src_ref=src, dst_ref=dst, send_sem=ssem, recv_sem=rsem,
            device_id=(g, dz, de),
            device_id_type=pl.DeviceIdType.MESH)

    rim = [
        remote(density.at[0], curs[0].at[nz, 0:ny], rim_send.at[0], rim_recv.at[0],
               jnp.maximum(d - 1, 0), e),
        remote(density.at[0, 0:8], curs[0].at[nz, ny:ny + 8], rim_send.at[1], rim_recv.at[1],
               jnp.maximum(d - 1, 0), 0),
        remote(density.at[:, 0:8], curs[0].at[0:nz, ny:ny + 8], rim_send.at[2], rim_recv.at[2],
               d, 0),
    ]
    sends_if = [d > 0, (d > 0) & (e == 1), e == 1]
    recvs_if = [d < peers - 1, (d < peers - 1) & (e == 0), e == 0]
    for copy, cond in zip(rim, sends_if):
        pl.when(cond)(copy.start)

    zero_row = jnp.zeros((nz, 8, plan0.x), F32)
    curs[0][:, ny + 8:ny + 16, :] = jnp.zeros((nz + 1, 8, plan0.x), F32)

    @pl.when(e == 1)
    def _():
        curs[0][0:nz, ny:ny + 8, :] = zero_row
        curs[0][nz, ny:ny + 8, :] = jnp.zeros((8, plan0.x), F32)

    @pl.when((e == 0) & (d == peers - 1))
    def _():
        curs[0][nz, ny:ny + 8, :] = jnp.zeros((8, plan0.x), F32)

    @pl.when(d == peers - 1)
    def _():
        curs[0][nz, 0:ny, :] = jnp.zeros((ny, plan0.x), F32)

    loads[0].wait()
    for copy, cond in zip(rim, recvs_if):
        pl.when(cond)(copy.wait_recv)

    a2a_all = []
    msg_all = []
    for l, plan in enumerate(plans):
        cur, mid, flat, send, prod = curs[l], mids[l], flats[l], sends[l], prods[l]
        z, y, x = plan.z, plan.y, plan.x
        lane = lax.broadcasted_iota(jnp.int32, (y + 8, x), 1)
        row = lax.broadcasted_iota(jnp.int32, (y + 8, x), 0)

        def widen(k, _, cur=cur, mid=mid, y=y, x=x, lane=lane, row=row):
            value = cur[2 * k, 0:y + 8, :]
            after = jnp.where(lane == x - 1, 0.0, pltpu.roll(value, x - 1, 1))
            value = jnp.where(lane % 2 == 1, (pltpu.roll(value, 1, 1) + after) * 0.5, value)
            both = pltpu.roll(value, 1, 0) + pltpu.roll(value, y + 7, 0)
            mid[k] = jnp.where(row % 2 == 1, both * 0.5, value)[0:y]
            return 0

        lax.fori_loop(0, plan.zc + 1, widen, 0)

        factor = scale[l]
        high, low = flat[0], flat[1]

        def subtract(k, _, cur=cur, mid=mid, y=y, high=high, low=low, flat=flat, plan=plan):
            here, there = mid[k], mid[k + 1]
            for odd in range(2):
                inter = (here + there) * 0.5 if odd else here
                detail = cur[2 * k + odd, 0:y, :] - inter
                at = pl.ds(pl.multiple_of((2 * k + odd) * y, y), y)
                quant = detail * factor
                if y % 16 == 0:
                    high[at, :], low[at, :] = split(detail)
                else:
                    high[at, :] = detail
                flat[2][at, :] = quant.astype(flat[2].dtype)
            return 0

        lax.fori_loop(0, plan.zc, subtract, 0)

        height = plan.piece if plan.packed else 8
        cols = lax.broadcasted_iota(jnp.int32, (height, z * y), 1)
        rows = lax.broadcasted_iota(jnp.int32, (height, z * y), 0)
        offset = cols - rows
        if not plan.packed:
            offset = jnp.where(rows < plan.piece, offset, -1)
        order = jnp.concatenate(
            [jnp.where(offset == inverse[l, w] * plan.piece, 1.0, 0.0) for w in range(peers)], axis=0)
        ordered = jnp.dot(order.astype(BF16), flat[2][...].astype(BF16), preferred_element_type=F32)
        send[...] = ordered.reshape(peers, height, x).astype(send.dtype)
        for s in range(1, peers):
            copy = remote(send.at[lax.rem(d + s, peers)], outs[l].at[d], a2a_send.at[l, s],
                          a2a_recv.at[l, s], lax.rem(d + s, peers), e)
            copy.start()
            a2a_all.append(copy)
        outs[l][d] = send[d]

        left = (high[...], low[...]) if y % 16 == 0 else split(high[...])
        inner = dot3(left, (col_w[l][0], col_w[l][1]))
        loads[1 + l].wait()
        prod[...] = dot3((row_w[l][0], row_w[l][1]), split(inner))

        messages = []
        for index, (dz, dy) in enumerate(plan.messages()):
            start, first, count, height = plan.blocks[dz, dy]
            target = jnp.clip(d + dz, 0, peers - 1)
            copy = remote(prod.at[start:start + count * height], slots[l][dz, dy],
                          msg_send.at[l, index], msg_recv.at[l, index],
                          target, e if dy == 0 else 1 - e)
            goes = (d + dz >= 0) & (d + dz < peers)
            comes = (d - dz >= 0) & (d - dz < peers)
            if dz == 0:
                copy.start()
            else:
                pl.when(goes)(copy.start)
            messages.append((copy, goes, comes, dz, dy))
        msg_all.extend(messages)

        br = plan.br
        target_ref = coarse_out if plan.last else curs[l + 1]
        strip = strips[l]
        for k in range(plan.kz):
            for b in range(x // 128):
                strip[b, k * 2 * br:(k + 1) * 2 * br, :] = cur[2 * k, 0:2 * br, b * 128:(b + 1) * 128]
        nodes = jnp.concatenate(
            [strip[b, pl.ds(0, plan.kz * br, stride=2), :] for b in range(x // 128)], axis=1)
        nh, nl = split(nodes)
        sel = sel_w[l][...]
        picked = (jnp.dot(nh, sel, preferred_element_type=F32)
                  + jnp.dot(nl, sel, preferred_element_type=F32))
        start = plan.blocks[0, 0][0]
        picked = picked + prod[start:start + plan.kz * br, :]
        for k in range(plan.kz):
            target_ref[k, 0:br, :] = picked[k * br:(k + 1) * br]
            if not plan.last:
                target_ref[k, br:br + 8, :] = jnp.zeros((8, plan.xc), F32)
        for copy, goes, comes, dz, dy in messages:
            _, first, count, height = plan.blocks[dz, dy]

            def add(copy=copy, dz=dz, dy=dy, first=first, count=count, height=height, l=l, plan=plan,
                    target_ref=target_ref):
                copy.wait_recv()
                slot = slots[l][dz, dy]
                for i in range(count):
                    got = slot[i * height:(i + 1) * height, :]
                    if dy == 0:
                        target_ref[first + i, 0:height, :] = target_ref[first + i, 0:height, :] + got
                    else:
                        low_row, span = plan.yc - 3, plan.jy - plan.yc + 3

                        @pl.when(e == 0)
                        def _():
                            target_ref[first + i, low_row:low_row + span, :] = (
                                target_ref[first + i, low_row:low_row + span, :] + got[0:span])

                        @pl.when(e == 1)
                        def _():
                            target_ref[first + i, 0:3, :] = target_ref[first + i, 0:3, :] + got[0:3]

            if dz == 0:
                add()
            else:
                pl.when(comes)(add)

    for copy, cond in zip(rim, sends_if):
        pl.when(cond)(copy.wait_send)
    for copy, goes, comes, dz, dy in msg_all:
        if dz == 0:
            copy.wait_send()
        else:
            pl.when(goes)(copy.wait_send)
    for copy in a2a_all:
        copy.wait()


def inverse_of(table):
    ids = jnp.arange(table.shape[1], dtype=jnp.int32)
    matches = (table[:, None, :] == ids[None, :, None]).astype(jnp.int32)
    return jnp.sum(matches * ids[None, None, :], axis=2)


def shards(density, bin_exponents, writer_table):
    peers, side = lax.axis_size("gz"), lax.axis_size("gy")
    nz, ny, nx = density.shape
    plans = [Plan(l, nz >> l, ny >> l, nx >> l, peers) for l in range(LEVELS)]
    row_w = [jnp.asarray(plan.rows_matrix(peers, side)) for plan in plans]
    col_w = [jnp.asarray(split_np(line_operator(plan.x).T)) for plan in plans]
    sel_w = [jnp.asarray(np.eye(plan.x)[:, ::2].astype(BF16)) for plan in plans]
    bin_scale = jnp.exp2(-bin_exponents.astype(F32))

    out_shape = [jax.ShapeDtypeStruct((plans[-1].zc, 8, plans[-1].xc), F32)]
    for plan in plans:
        if plan.packed:
            out_shape.append(jax.ShapeDtypeStruct((peers, plan.piece, plan.x), BF16))
        else:
            out_shape.append(jax.ShapeDtypeStruct((peers, 8, plan.x), F32))

    scratch = []
    scratch += [pltpu.VMEM((p.z + 1, p.y + 16, p.x), F32) for p in plans]
    scratch += [pltpu.VMEM((2, p.m, p.z * p.y), BF16) for p in plans]
    scratch += [pltpu.VMEM((p.zc + 1, p.y, p.x), F32) for p in plans]
    for p in plans:
        scratch.append([pltpu.VMEM((p.z * p.y, p.x), BF16 if p.y % 16 == 0 else F32)] * 3)
    for shape in out_shape[1:]:
        scratch.append(pltpu.VMEM(shape.shape, shape.dtype))
    scratch += [pltpu.VMEM((p.m, p.xc), F32) for p in plans]
    scratch += [pltpu.VMEM((p.x // 128, p.kz * 2 * p.br, 128), F32) for p in plans]
    for p in plans:
        for key in p.messages():
            _, _, count, height = p.blocks[key]
            scratch.append(pltpu.VMEM((count * height, p.xc), F32))
    most = max(len(p.messages()) for p in plans)
    scratch += [pltpu.SemaphoreType.DMA((1 + LEVELS,))]
    scratch += [pltpu.SemaphoreType.DMA((3,))] * 2
    scratch += [pltpu.SemaphoreType.DMA((LEVELS, most))] * 2
    scratch += [pltpu.SemaphoreType.DMA((LEVELS, peers))] * 2

    vmem, smem, hbm = (pl.BlockSpec(memory_space=s) for s in (pltpu.VMEM, pltpu.SMEM, pl.ANY))
    outputs = pl.pallas_call(
        functools.partial(kernel, plans, peers),
        out_shape=out_shape,
        in_specs=[hbm, smem, smem] + [hbm] * LEVELS + [vmem] * (2 * LEVELS),
        out_specs=[vmem] * (1 + LEVELS),
        scratch_shapes=scratch,
        compiler_params=pltpu.CompilerParams(
            collective_id=0, has_side_effects=True, vmem_limit_bytes=56 * 1024 * 1024),
        cost_estimate=pl.CostEstimate(flops=10**9, bytes_accessed=10**7, transcendentals=0),
    )(density, bin_scale, inverse_of(writer_table), *row_w, *col_w, *sel_w)
    coarse = outputs[0][:, 0:plans[-1].yc, :]
    results = [coarse]
    for plan, value in zip(plans, outputs[1:]):
        if not plan.packed:
            value = value[:, 0:plan.piece, :].astype(BF16)
        results.append(value.reshape(1, 1, peers, -1))
    return tuple(results)


def solution(mesh):
    in_specs = (P(("grp", "gz"), "gy", None), P(), P())
    out_specs = (
        P(("grp", "gz"), "gy", None),
        P(("grp", "gz"), "gy", None, None),
        P(("grp", "gz"), "gy", None, None),
        P(("grp", "gz"), "gy", None, None),
    )
    return jax.shard_map(shards, mesh=mesh, in_specs=in_specs, out_specs=out_specs, check_vma=False)
```

time: 597 us -> 68.6 us (0.11); the launches traced: 587 us -> 68.3 us
  local copies, waits for them, and re-layouts: 369 us -> 7.05 us
  starting transfers between devices: 100 us -> 0 us
  waiting for transfers between devices: 73.9 us -> 0 us
  Pallas kernels: 0 us -> 58.1 us
  other arithmetic: 39.8 us -> 2.58 us
    slice x58 -> x2, local copies, waits for them, and re-layouts: 346 us -> 2.14 us  [the longest x1 1.29 us: shards(): coarse = outputs[0][:, 0:plans[-1].yc, :]]
    ppermute x42 -> x0, starting transfers between devices: 85.9 us -> none  [the longest x18 54.4 us: extended_2(): before = lax.ppermute(last, axis, up)]
    ppermute x42 -> x0, waiting for transfers between devices: 66.3 us -> none  [the longest x18 45.4 us: extended_2(): after = lax.ppermute(initial, axis, down)]
    pallas_call x0 -> x1, Pallas kernels: none -> 58.1 us  [shards(): pl.pallas_call(functools.partial(kernel, plans, peers), out_shape=out_sha...]
    another operation x18 -> x0, other arithmetic: 14.2 us -> none  [upsample(): stacked = jnp.stack((lower_part, middle), axis=dim_index + 1)]
    all_to_all x3 -> x0, starting transfers between devices: 14.1 us -> none  [shards(): lax.all_to_all(message, 'gz', split_axis=2, concat_axis=2, tiled=True)]
    another operation x10 -> x0, local copies, waits for them, and re-layouts: 9.43 us -> none  [upsample(): stacked = jnp.stack((lower_part, middle), axis=dim_index + 1)]
    unnamed x4 -> x0, other arithmetic: 9.23 us -> none
  transfers between devices with their start and end apart: 45 -> 0, of which waited for: 25 -> 0; matrix products, arithmetic and copies ran while one was open for 5% -> 0% of each run, Pallas kernels for 0% -> 0%
where the time goes in v1:
time: 68.6 us; the launch traced here: 68.3 us
  Pallas kernels  58.1 us (85%)
  local copies, waits for them, and re-layouts  7.05 us (10%)
  other arithmetic  2.58 us (4%)
    pallas_call x1, Pallas kernels, shards(): pl.pallas_call(functools.partial(kernel, plans, peers), out_shape=out_sha...  58.1 us
    reshape x3, local copies, waits for them, and re-layouts, shards(): results.append(value.reshape(1, 1, peers, -1))  4.91 us
    reduce_sum x1, other arithmetic, inverse_of(): return jnp.sum(matches * ids[None, None, :], axis=2)  1.41 us

profile of v1, /device:TPU:0, one launch (start us, length us, event | category | flops | bytes accessed | tf_op | source)
XLA Modules:
  0.0 68.3 jit_solution(5097845683264126936)
XLA Ops:
  0.6 1.2 %multiply_exponential_fusion.scale = f32[3]{0:T(128)} fusion(s32[3]{0:T(128)} %param.13), kind=kLoop, calls=%fused_computation.3 | loop fusion | flops 9 | bytes 24 | tf_op jit(solution)/shard_map/exp2 | solution.py:312
  1.8 1.4 %select_reduce_fusion.inverse = s32[3,8]{1,0:T(4,128)} fusion(s32[3,8]{1,0:T(4,128)} %param.14), kind=kLoop, calls=%fused_computation.1 | loop fusion | flops 552 | bytes 192 | tf_op jit(solution)/shard_map/reduce_sum | solution.py:302
  3.2 58.1 %shard_map.147 = (f32[2,8,128]{2,1,0:T(8,128)}, bf16[8,64,1024]{2,1,0:T(8,128)(2,1)}, bf16[8,16,512]{2,1,0:T(8,128)(2,1)}, f32[8,8,256]{2,1,0:T(8,128)}) custom-call(f32[16,32,1024]{2,1,0:T(8,128)} %density.1, f32[3]{0:T(128)} %multiply_exponential_fusion.scale, s32[3,8]{1,0:T(4,128)} %select_reduce_fusion.inverse, ...), custom_call_target="tpu_custom_call" | custom-call | flops 1000000000 | bytes 10000000 | tf_op jit(solution)/shard_map/pallas_call | solution.py:342
  61.3 1.3 %slice.7 = f32[2,4,128]{2,1,0:T(4,128)} slice(f32[2,8,128]{2,1,0:T(8,128)} %get-tuple-element.8), slice={[0:2], [0:4], [0:128]} | slice | bytes 8192 | tf_op jit(solution)/shard_map/slice | solution.py:352
  62.6 0.8 %slice.11 = bf16[8,4,256]{2,1,0:T(4,128)(2,1)S(1)} slice(f32[8,8,256]{2,1,0:T(8,128)} %get-tuple-element.11), slice={[0:8], [0:4], [0:256]} | slice | bytes 32768 | tf_op jit(solution)/shard_map/slice | solution.py:356
  63.4 0.6 reshape.20
  64.0 1.6 %reshape.19 = bf16[1,1,8,8192]{3,2,1,0:T(8,128)(2,1)} reshape(bf16[8,16,512]{2,1,0:T(8,128)(2,1)} %get-tuple-element.10) | data formatting | bytes 262144 | tf_op jit(solution)/shard_map/reshape | solution.py:357
  65.7 2.7 %reshape.18 = bf16[1,1,8,65536]{3,2,1,0:T(8,128)(2,1)} reshape(bf16[8,64,1024]{2,1,0:T(8,128)(2,1)} %get-tuple-element.9) | data formatting | bytes 2097152 | tf_op jit(solution)/shard_map/reshape | solution.py:357

commit v2 on v1

--- a/solution.py
+++ b/solution.py
@@ -95,24 +95,29 @@
         return np.stack(out)
 
 
-def kernel(plans, peers, density, scale, inverse, *refs):
+def kernel(plans, peers, density, exponents, table, *refs):
     refs = list(refs)
     take = lambda count: [refs.pop(0) for _ in range(count)]
-    row_hbm, col_w, sel_w = take(LEVELS), take(LEVELS), take(LEVELS)
+    row_hbm, col_hbm, sel_hbm = take(LEVELS), take(LEVELS), take(LEVELS)
     coarse_out = refs.pop(0)
     outs = take(LEVELS)
-    curs, row_w, mids, flats, sends, prods, strips = (take(LEVELS) for _ in range(7))
+    curs, row_w, mids, flats, sends, prods, strips, col_w, sel_w, gathers = (take(LEVELS) for _ in range(10))
     slots = [{key: refs.pop(0) for key in plan.messages()} for plan in plans]
-    local_sem, rim_send, rim_recv, msg_send, msg_recv, a2a_send, a2a_recv = refs
+    coarse_full, local_sem, rim_send, rim_recv, msg_send, msg_recv, a2a_send, a2a_recv = refs
 
     g, d, e = lax.axis_index("grp"), lax.axis_index("gz"), lax.axis_index("gy")
+    def inverse(l, w):
+        return sum(jnp.where(table[l, p] == w, p, 0) for p in range(peers))
+
     variant = ((d + peers - 1) // peers + d // (peers - 1)) * 2 + e
     plan0 = plans[0]
     nz, ny = plan0.z, plan0.y
 
     loads = [pltpu.make_async_copy(density, curs[0].at[0:nz, 0:ny], local_sem.at[0])]
     for l in range(LEVELS):
-        loads.append(pltpu.make_async_copy(row_hbm[l].at[variant], row_w[l], local_sem.at[1 + l]))
+        loads.append(pltpu.make_async_copy(row_hbm[l].at[variant], row_w[l], local_sem.at[1 + 3 * l]))
+        loads.append(pltpu.make_async_copy(col_hbm[l], col_w[l], local_sem.at[2 + 3 * l]))
+        loads.append(pltpu.make_async_copy(sel_hbm[l], sel_w[l], local_sem.at[3 + 3 * l]))
     for load in loads:
         load.start()
 
@@ -161,10 +166,9 @@
         curs[0][nz, 0:ny, :] = jnp.zeros((ny, plan0.x), F32)
 
     loads[0].wait()
-    for copy, cond in zip(rim, recvs_if):
-        pl.when(cond)(copy.wait_recv)
-
-    a2a_all = []
+    pl.when(recvs_if[2])(rim[2].wait_recv)
+
+    a2a_all = [[] for _ in range(LEVELS)]
     msg_all = []
     for l, plan in enumerate(plans):
         cur, mid, flat, send, prod = curs[l], mids[l], flats[l], sends[l], prods[l]
@@ -180,9 +184,13 @@
             mid[k] = jnp.where(row % 2 == 1, both * 0.5, value)[0:y]
             return 0
 
-        lax.fori_loop(0, plan.zc + 1, widen, 0)
-
-        factor = scale[l]
+        lax.fori_loop(0, plan.zc, widen, 0)
+        if l > 0:
+            widen(plan.zc, 0)
+
+        factor = jnp.float32(1.0)
+        for power in range(-4, 5):
+            factor = jnp.where(exponents[l] == power, 2.0 ** -power, factor)
         high, low = flat[0], flat[1]
 
         def subtract(k, _, cur=cur, mid=mid, y=y, high=high, low=low, flat=flat, plan=plan):
@@ -199,7 +207,14 @@
                 flat[2][at, :] = quant.astype(flat[2].dtype)
             return 0
 
-        lax.fori_loop(0, plan.zc, subtract, 0)
+        if l > 0:
+            lax.fori_loop(0, plan.zc, subtract, 0)
+        else:
+            lax.fori_loop(0, plan.zc - 1, subtract, 0)
+            pl.when(recvs_if[0])(rim[0].wait_recv)
+            pl.when(recvs_if[1])(rim[1].wait_recv)
+            widen(plan.zc, 0)
+            subtract(plan.zc - 1, 0)
 
         height = plan.piece if plan.packed else 8
         cols = lax.broadcasted_iota(jnp.int32, (height, z * y), 1)
@@ -208,19 +223,20 @@
         if not plan.packed:
             offset = jnp.where(rows < plan.piece, offset, -1)
         order = jnp.concatenate(
-            [jnp.where(offset == inverse[l, w] * plan.piece, 1.0, 0.0) for w in range(peers)], axis=0)
+            [jnp.where(offset == inverse(l, w) * plan.piece, 1.0, 0.0) for w in range(peers)], axis=0)
         ordered = jnp.dot(order.astype(BF16), flat[2][...].astype(BF16), preferred_element_type=F32)
         send[...] = ordered.reshape(peers, height, x).astype(send.dtype)
         for s in range(1, peers):
-            copy = remote(send.at[lax.rem(d + s, peers)], outs[l].at[d], a2a_send.at[l, s],
+            copy = remote(send.at[lax.rem(d + s, peers)], gathers[l].at[d], a2a_send.at[l, s],
                           a2a_recv.at[l, s], lax.rem(d + s, peers), e)
             copy.start()
-            a2a_all.append(copy)
-        outs[l][d] = send[d]
-
+            a2a_all[l].append(copy)
+        gathers[l][d] = send[d]
+
+        for load in loads[1 + 3 * l:4 + 3 * l]:
+            load.wait()
         left = (high[...], low[...]) if y % 16 == 0 else split(high[...])
         inner = dot3(left, (col_w[l][0], col_w[l][1]))
-        loads[1 + l].wait()
         prod[...] = dot3((row_w[l][0], row_w[l][1]), split(inner))
 
         messages = []
@@ -240,7 +256,7 @@
         msg_all.extend(messages)
 
         br = plan.br
-        target_ref = coarse_out if plan.last else curs[l + 1]
+        target_ref = coarse_full if plan.last else curs[l + 1]
         strip = strips[l]
         for k in range(plan.kz):
             for b in range(x // 128):
@@ -292,14 +308,21 @@
             copy.wait_send()
         else:
             pl.when(goes)(copy.wait_send)
-    for copy in a2a_all:
-        copy.wait()
-
-
-def inverse_of(table):
-    ids = jnp.arange(table.shape[1], dtype=jnp.int32)
-    matches = (table[:, None, :] == ids[None, :, None]).astype(jnp.int32)
-    return jnp.sum(matches * ids[None, None, :], axis=2)
+    coarse_out[...] = coarse_full[:, 0:plans[-1].yc, :]
+
+    for l in reversed(range(LEVELS)):
+        for copy in a2a_all[l]:
+            copy.wait()
+        plan = plans[l]
+        height = plan.piece if plan.packed else 8
+        count = plan.piece * peers
+        to = lax.broadcasted_iota(jnp.int32, (count, peers * height), 0)
+        at = lax.broadcasted_iota(jnp.int32, (count, peers * height), 1)
+        turn = jnp.where(at == to % peers * height + to // peers, 1.0, 0.0).astype(BF16)
+        turned = jnp.dot(turn, gathers[l][...].reshape(peers * height, plan.x).astype(BF16),
+                         preferred_element_type=F32).astype(BF16)
+        for r in range(plan.piece):
+            outs[l][0, 0, :, r * plan.x:(r + 1) * plan.x] = turned[r * peers:(r + 1) * peers]
 
 
 def shards(density, bin_exponents, writer_table):
@@ -309,14 +332,10 @@
     row_w = [jnp.asarray(plan.rows_matrix(peers, side)) for plan in plans]
     col_w = [jnp.asarray(split_np(line_operator(plan.x).T)) for plan in plans]
     sel_w = [jnp.asarray(np.eye(plan.x)[:, ::2].astype(BF16)) for plan in plans]
-    bin_scale = jnp.exp2(-bin_exponents.astype(F32))
-
-    out_shape = [jax.ShapeDtypeStruct((plans[-1].zc, 8, plans[-1].xc), F32)]
+
+    out_shape = [jax.ShapeDtypeStruct((plans[-1].zc, plans[-1].yc, plans[-1].xc), F32)]
     for plan in plans:
-        if plan.packed:
-            out_shape.append(jax.ShapeDtypeStruct((peers, plan.piece, plan.x), BF16))
-        else:
-            out_shape.append(jax.ShapeDtypeStruct((peers, 8, plan.x), F32))
+        out_shape.append(jax.ShapeDtypeStruct((1, 1, peers, plan.piece * plan.x), BF16))
 
     scratch = []
     scratch += [pltpu.VMEM((p.z + 1, p.y + 16, p.x), F32) for p in plans]
@@ -324,38 +343,36 @@
     scratch += [pltpu.VMEM((p.zc + 1, p.y, p.x), F32) for p in plans]
     for p in plans:
         scratch.append([pltpu.VMEM((p.z * p.y, p.x), BF16 if p.y % 16 == 0 else F32)] * 3)
-    for shape in out_shape[1:]:
-        scratch.append(pltpu.VMEM(shape.shape, shape.dtype))
+    scratch += [pltpu.VMEM((peers, p.piece if p.packed else 8, p.x), BF16 if p.packed else F32)
+                for p in plans]
     scratch += [pltpu.VMEM((p.m, p.xc), F32) for p in plans]
     scratch += [pltpu.VMEM((p.x // 128, p.kz * 2 * p.br, 128), F32) for p in plans]
+    scratch += [pltpu.VMEM((2, p.x, p.xc), BF16) for p in plans]
+    scratch += [pltpu.VMEM((p.x, p.xc), BF16) for p in plans]
+    scratch += [pltpu.VMEM((peers, p.piece if p.packed else 8, p.x), BF16 if p.packed else F32)
+                for p in plans]
     for p in plans:
         for key in p.messages():
             _, _, count, height = p.blocks[key]
             scratch.append(pltpu.VMEM((count * height, p.xc), F32))
     most = max(len(p.messages()) for p in plans)
-    scratch += [pltpu.SemaphoreType.DMA((1 + LEVELS,))]
+    scratch.append(pltpu.VMEM((plans[-1].zc, 8, plans[-1].xc), F32))
+    scratch += [pltpu.SemaphoreType.DMA((1 + 3 * LEVELS,))]
     scratch += [pltpu.SemaphoreType.DMA((3,))] * 2
     scratch += [pltpu.SemaphoreType.DMA((LEVELS, most))] * 2
     scratch += [pltpu.SemaphoreType.DMA((LEVELS, peers))] * 2
 
     vmem, smem, hbm = (pl.BlockSpec(memory_space=s) for s in (pltpu.VMEM, pltpu.SMEM, pl.ANY))
-    outputs = pl.pallas_call(
+    return tuple(pl.pallas_call(
         functools.partial(kernel, plans, peers),
         out_shape=out_shape,
-        in_specs=[hbm, smem, smem] + [hbm] * LEVELS + [vmem] * (2 * LEVELS),
+        in_specs=[hbm, smem, smem] + [hbm] * (3 * LEVELS),
         out_specs=[vmem] * (1 + LEVELS),
         scratch_shapes=scratch,
         compiler_params=pltpu.CompilerParams(
             collective_id=0, has_side_effects=True, vmem_limit_bytes=56 * 1024 * 1024),
         cost_estimate=pl.CostEstimate(flops=10**9, bytes_accessed=10**7, transcendentals=0),
-    )(density, bin_scale, inverse_of(writer_table), *row_w, *col_w, *sel_w)
-    coarse = outputs[0][:, 0:plans[-1].yc, :]
-    results = [coarse]
-    for plan, value in zip(plans, outputs[1:]):
-        if not plan.packed:
-            value = value[:, 0:plan.piece, :].astype(BF16)
-        results.append(value.reshape(1, 1, peers, -1))
-    return tuple(results)
+    )(density, bin_exponents, writer_table, *row_w, *col_w, *sel_w))
 
 
 def solution(mesh):

time: 68.6 us -> 61.6 us (0.90)
  other arithmetic: 2.58 us -> 0 us
  local copies, waits for them, and re-layouts: 7.05 us -> 4.84 us
  Pallas kernels: 58.1 us -> 55.9 us
    reshape x3 -> x0, local copies, waits for them, and re-layouts: 4.91 us -> none  [shards(): results.append(value.reshape(1, 1, peers, -1))]
    unnamed x0 -> x8, local copies, waits for them, and re-layouts: none -> 4.84 us
    slice x2 -> x0, local copies, waits for them, and re-layouts: 2.14 us -> none  [the longest x1 1.29 us: shards(): coarse = outputs[0][:, 0:plans[-1].yc, :]]
    pallas_call x1, Pallas kernels: 58.1 us -> 55.9 us  [shards(): pl.pallas_call(functools.partial(kernel, plans, peers), out_shape=out_sha...]
    reduce_sum x1 -> x0, other arithmetic: 1.41 us -> none  [inverse_of(): return jnp.sum(matches * ids[None, None, :], axis=2)]
    exp2 x1 -> x0, other arithmetic: 1.18 us -> none  [shards(): bin_scale = jnp.exp2(-bin_exponents.astype(F32))]
where the time goes in v2:
time: 61.6 us; the launch traced here: 61.4 us
  Pallas kernels  55.9 us (91%)
  local copies, waits for them, and re-layouts  4.84 us (8%)
  between operations  0.66 us (1%)
    pallas_call x1, Pallas kernels, shards(): pl.pallas_call(functools.partial(kernel, plans, peers), out_shape=out_sha...  55.9 us
    unnamed x8, local copies, waits for them, and re-layouts  4.84 us

profile of v2, /device:TPU:0, one launch (start us, length us, event | category | flops | bytes accessed | tf_op | source)
XLA Modules:
  0.0 61.4 jit_solution(12444436117814168856)
XLA Ops:
  0.6 55.9 %shard_map.147 = (f32[2,4,128]{2,1,0:T(4,128)}, bf16[1,1,8,65536]{3,2,1,0:T(8,128)(2,1)}, bf16[1,1,8,8192]{3,2,1,0:T(8,128)(2,1)}, bf16[1,1,8,1024]{3,2,1,0:T(8,128)(2,1)}) custom-call(f32[16,32,1024]{2,1,0:T(8,128)} %density.1, s32[3]{0:T(128)} %exponents.1, s32[3,8]{1,0:T(4,128)} %table.1, bf16[6,2,512,512]{3,2,1,0:T(8,128)(2,1)} %constant.18.clone.refs_0_, ...), custom_call_target="tpu_custom_call" | custom-call | flops 1000000000 | bytes 10000000 | tf_op jit(solution)/shard_map/pallas_call | solution.py:366
  56.6 0.0 copy-start
  56.6 0.0 copy-start.1
  56.6 1.3 %copy.20 = f32[2,4,128]{2,1,0:T(4,128)} copy(f32[2,4,128]{2,1,0:T(4,128)} %get-tuple-element.8) | data formatting | bytes 8192
  57.9 2.3 %copy.21 = bf16[1,1,8,65536]{3,2,1,0:T(8,128)(2,1)} copy(bf16[1,1,8,65536]{3,2,1,0:T(8,128)(2,1)} %get-tuple-element.9) | data formatting | bytes 2097152
  60.2 0.0 copy-done
  60.2 0.7 %copy.22 = bf16[1,1,8,8192]{3,2,1,0:T(8,128)(2,1)} copy(bf16[1,1,8,8192]{3,2,1,0:T(8,128)(2,1)S(1)} %copy-done) | data formatting | bytes 262144
  60.8 0.0 copy-done.1
  60.8 0.6 copy.23
Async XLA Ops:
  56.6 3.6 %copy-start = (bf16[1,1,8,8192]{3,2,1,0:T(8,128)(2,1)S(1)}, bf16[1,1,8,8192]{3,2,1,0:T(8,128)(2,1)}, u32[]{:S(2)}) copy-start(bf16[1,1,8,8192]{3,2,1,0:T(8,128)(2,1)} %get-tuple-element.10) | copy-start | bytes 393220
  56.6 4.2 %copy-start.1 = (bf16[1,1,8,1024]{3,2,1,0:T(8,128)(2,1)S(1)}, bf16[1,1,8,1024]{3,2,1,0:T(8,128)(2,1)}, u32[]{:S(2)}) copy-start(bf16[1,1,8,1024]{3,2,1,0:T(8,128)(2,1)} %get-tuple-element.11) | copy-start | bytes 49156

commit v3 on v2

--- a/solution.py
+++ b/solution.py
@@ -62,9 +62,14 @@
             if not ks:
                 continue
             for dy in (0, 1):
-                height = self.br if dy == 0 else 8
-                self.blocks[dz, dy] = (total, ks[0], len(ks), height)
-                total += len(ks) * height
+                if dy == 1:
+                    height, size = 4, -(-len(ks) * 4 // 8) * 8
+                elif dz == 0 or self.last:
+                    height, size = self.br, len(ks) * self.br
+                else:
+                    height, size = self.yc, len(ks) * self.yc + 8
+                self.blocks[dz, dy] = (total, ks[0], len(ks), height, size)
+                total += size
         self.m = total
 
     def messages(self):
@@ -76,7 +81,7 @@
         for d in (0, peers // 2, peers - 1):
             for e in range(side):
                 full = np.zeros((self.m, self.z * self.y))
-                for (dz, dy), (start, first, count, height) in self.blocks.items():
+                for (dz, dy), (start, first, count, height, _) in self.blocks.items():
                     dest = e if dy == 0 else 1 - e
                     base = 0 if dy == 0 or dest == 1 else self.yc - 3
                     span = self.jy if dy == 0 else (3 if dest == 1 else self.jy - base)
@@ -90,12 +95,15 @@
                             if gj >= self.yc * side:
                                 continue
                             yrow = ya[gj, e * self.y:(e + 1) * self.y]
-                            full[start + i * height + j] = np.kron(zrow, yrow)
+                            at = start + i * height + j
+                            if dy == 0 and dz != 0 and j >= height:
+                                at = start + count * height + i
+                            full[at] = np.kron(zrow, yrow)
                 out.append(split_np(full))
         return np.stack(out)
 
 
-def kernel(plans, peers, density, exponents, table, *refs):
+def kernel(plans, peers, density, paired, exponents, table, *refs):
     refs = list(refs)
     take = lambda count: [refs.pop(0) for _ in range(count)]
     row_hbm, col_hbm, sel_hbm = take(LEVELS), take(LEVELS), take(LEVELS)
@@ -103,7 +111,7 @@
     outs = take(LEVELS)
     curs, row_w, mids, flats, sends, prods, strips, col_w, sel_w, gathers = (take(LEVELS) for _ in range(10))
     slots = [{key: refs.pop(0) for key in plan.messages()} for plan in plans]
-    coarse_full, local_sem, rim_send, rim_recv, msg_send, msg_recv, a2a_send, a2a_recv = refs
+    coarse_full, row_rim, local_sem, rim_send, rim_recv, msg_send, msg_recv, a2a_send, a2a_recv = refs
 
     g, d, e = lax.axis_index("grp"), lax.axis_index("gz"), lax.axis_index("gy")
     def inverse(l, w):
@@ -141,7 +149,7 @@
                jnp.maximum(d - 1, 0), e),
         remote(density.at[0, 0:8], curs[0].at[nz, ny:ny + 8], rim_send.at[1], rim_recv.at[1],
                jnp.maximum(d - 1, 0), 0),
-        remote(density.at[:, 0:8], curs[0].at[0:nz, ny:ny + 8], rim_send.at[2], rim_recv.at[2],
+        remote(paired.at[:, 0, 0:8], row_rim, rim_send.at[2], rim_recv.at[2],
                d, 0),
     ]
     sends_if = [d > 0, (d > 0) & (e == 1), e == 1]
@@ -166,10 +174,16 @@
         curs[0][nz, 0:ny, :] = jnp.zeros((ny, plan0.x), F32)
 
     loads[0].wait()
-    pl.when(recvs_if[2])(rim[2].wait_recv)
+    @pl.when(recvs_if[2])
+    def _():
+        rim[2].wait_recv()
+        for k in range(nz // 2):
+            curs[0][2 * k, ny:ny + 8, :] = row_rim[k]
+
 
     a2a_all = [[] for _ in range(LEVELS)]
     msg_all = []
+    far_first = sorted(range(1, peers), key=lambda s: abs(2 * s - peers))
     for l, plan in enumerate(plans):
         cur, mid, flat, send, prod = curs[l], mids[l], flats[l], sends[l], prods[l]
         z, y, x = plan.z, plan.y, plan.x
@@ -229,7 +243,6 @@
         for s in range(1, peers):
             copy = remote(send.at[lax.rem(d + s, peers)], gathers[l].at[d], a2a_send.at[l, s],
                           a2a_recv.at[l, s], lax.rem(d + s, peers), e)
-            copy.start()
             a2a_all[l].append(copy)
         gathers[l][d] = send[d]
 
@@ -241,9 +254,9 @@
 
         messages = []
         for index, (dz, dy) in enumerate(plan.messages()):
-            start, first, count, height = plan.blocks[dz, dy]
+            start, size = plan.blocks[dz, dy][0], plan.blocks[dz, dy][4]
             target = jnp.clip(d + dz, 0, peers - 1)
-            copy = remote(prod.at[start:start + count * height], slots[l][dz, dy],
+            copy = remote(prod.at[start:start + size], slots[l][dz, dy],
                           msg_send.at[l, index], msg_recv.at[l, index],
                           target, e if dy == 0 else 1 - e)
             goes = (d + dz >= 0) & (d + dz < peers)
@@ -254,6 +267,11 @@
                 pl.when(goes)(copy.start)
             messages.append((copy, goes, comes, dz, dy))
         msg_all.extend(messages)
+        if l > 0:
+            for copy in a2a_all[l]:
+                copy.start()
+        for index in range(l, peers - 1, LEVELS):
+            a2a_all[0][far_first[index] - 1].start()
 
         br = plan.br
         target_ref = coarse_full if plan.last else curs[l + 1]
@@ -274,7 +292,7 @@
             if not plan.last:
                 target_ref[k, br:br + 8, :] = jnp.zeros((8, plan.xc), F32)
         for copy, goes, comes, dz, dy in messages:
-            _, first, count, height = plan.blocks[dz, dy]
+            _, first, count, height, _ = plan.blocks[dz, dy]
 
             def add(copy=copy, dz=dz, dy=dy, first=first, count=count, height=height, l=l, plan=plan,
                     target_ref=target_ref):
@@ -284,6 +302,10 @@
                     got = slot[i * height:(i + 1) * height, :]
                     if dy == 0:
                         target_ref[first + i, 0:height, :] = target_ref[first + i, 0:height, :] + got
+                        if dz != 0 and not plan.last:
+                            edge, at = plan.yc, count * height + i
+                            target_ref[first + i, edge:edge + 1, :] = (
+                                target_ref[first + i, edge:edge + 1, :] + slot[at:at + 1, :])
                     else:
                         low_row, span = plan.yc - 3, plan.jy - plan.yc + 3
 
@@ -353,10 +375,10 @@
                 for p in plans]
     for p in plans:
         for key in p.messages():
-            _, _, count, height = p.blocks[key]
-            scratch.append(pltpu.VMEM((count * height, p.xc), F32))
+            scratch.append(pltpu.VMEM((p.blocks[key][4], p.xc), F32))
     most = max(len(p.messages()) for p in plans)
     scratch.append(pltpu.VMEM((plans[-1].zc, 8, plans[-1].xc), F32))
+    scratch.append(pltpu.VMEM((nz // 2, 8, nx), F32))
     scratch += [pltpu.SemaphoreType.DMA((1 + 3 * LEVELS,))]
     scratch += [pltpu.SemaphoreType.DMA((3,))] * 2
     scratch += [pltpu.SemaphoreType.DMA((LEVELS, most))] * 2
@@ -366,13 +388,13 @@
     return tuple(pl.pallas_call(
         functools.partial(kernel, plans, peers),
         out_shape=out_shape,
-        in_specs=[hbm, smem, smem] + [hbm] * (3 * LEVELS),
+        in_specs=[hbm, hbm, smem, smem] + [hbm] * (3 * LEVELS),
         out_specs=[vmem] * (1 + LEVELS),
         scratch_shapes=scratch,
         compiler_params=pltpu.CompilerParams(
             collective_id=0, has_side_effects=True, vmem_limit_bytes=56 * 1024 * 1024),
         cost_estimate=pl.CostEstimate(flops=10**9, bytes_accessed=10**7, transcendentals=0),
-    )(density, bin_exponents, writer_table, *row_w, *col_w, *sel_w))
+    )(density, density.reshape(nz // 2, 2, ny, nx), bin_exponents, writer_table, *row_w, *col_w, *sel_w))
 
 
 def solution(mesh):

time: 61.6 us -> 55.7 us (0.904); the launches traced: 61.4 us -> 54.8 us
  Pallas kernels: 55.9 us -> 49.3 us
    pallas_call x1, Pallas kernels: 55.9 us -> 49.3 us  [shards(): pl.pallas_call(functools.partial(kernel, plans, peers), out_shape=out_sha...]
where the time goes in v3:
time: 55.7 us; the launch traced here: 54.8 us
  Pallas kernels  49.3 us (89%)
  local copies, waits for them, and re-layouts  4.84 us (9%)
  between operations  0.66 us (1%)
    pallas_call x1, Pallas kernels, shards(): pl.pallas_call(functools.partial(kernel, plans, peers), out_shape=out_sha...  49.3 us
    unnamed x8, local copies, waits for them, and re-layouts  4.84 us

profile of v3, /device:TPU:0, one launch (start us, length us, event | category | flops | bytes accessed | tf_op | source)
XLA Modules:
  0.0 54.8 jit_solution(9507048649780337297)
XLA Ops:
  0.6 49.3 %shard_map.147 = (f32[2,4,128]{2,1,0:T(4,128)}, bf16[1,1,8,65536]{3,2,1,0:T(8,128)(2,1)}, bf16[1,1,8,8192]{3,2,1,0:T(8,128)(2,1)}, bf16[1,1,8,1024]{3,2,1,0:T(8,128)(2,1)}) custom-call(f32[16,32,1024]{2,1,0:T(8,128)} %density.1, f32[8,2,32,1024]{3,2,1,0:T(8,128)} %bitcast.1, s32[3]{0:T(128)} %exponents.1, s32[3,8]{1,0:T(4,128)} %table.1, ...), custom_call_target="tpu_custom_call" | custom-call | flops 1000000000 | bytes 10000000 | tf_op jit(solution)/shard_map/pallas_call | solution.py:388
  50.0 0.0 copy-start
  50.0 0.0 copy-start.1
  50.0 1.3 %copy.20 = f32[2,4,128]{2,1,0:T(4,128)} copy(f32[2,4,128]{2,1,0:T(4,128)} %get-tuple-element.8) | data formatting | bytes 8192
  51.3 2.3 %copy.21 = bf16[1,1,8,65536]{3,2,1,0:T(8,128)(2,1)} copy(bf16[1,1,8,65536]{3,2,1,0:T(8,128)(2,1)} %get-tuple-element.9) | data formatting | bytes 2097152
  53.6 0.0 copy-done
  53.6 0.7 %copy.22 = bf16[1,1,8,8192]{3,2,1,0:T(8,128)(2,1)} copy(bf16[1,1,8,8192]{3,2,1,0:T(8,128)(2,1)S(1)} %copy-done) | data formatting | bytes 262144
  54.2 0.0 copy-done.1
  54.2 0.6 %copy.23 = bf16[1,1,8,1024]{3,2,1,0:T(8,128)(2,1)} copy(bf16[1,1,8,1024]{3,2,1,0:T(8,128)(2,1)S(1)} %copy-done.1) | data formatting | bytes 32768
Async XLA Ops:
  50.0 3.6 %copy-start = (bf16[1,1,8,8192]{3,2,1,0:T(8,128)(2,1)S(1)}, bf16[1,1,8,8192]{3,2,1,0:T(8,128)(2,1)}, u32[]{:S(2)}) copy-start(bf16[1,1,8,8192]{3,2,1,0:T(8,128)(2,1)} %get-tuple-element.10) | copy-start | bytes 393220
  50.0 4.2 %copy-start.1 = (bf16[1,1,8,1024]{3,2,1,0:T(8,128)(2,1)S(1)}, bf16[1,1,8,1024]{3,2,1,0:T(8,128)(2,1)}, u32[]{:S(2)}) copy-start(bf16[1,1,8,1024]{3,2,1,0:T(8,128)(2,1)} %get-tuple-element.11) | copy-start | bytes 49156
